TPU v7x, 128 devices: a whole 4x4x4 slice. The times are simulated.
128 devices in a mesh: ctx: 32 (over z, y, core), tp: 4 (over x).
Axes of the slice: x: 4, y: 4, z: 4, core: 2. Of those that a mesh axis runs over, the one named last changes fastest.
Arguments:
- x_tokens: bfloat16 [16384, 4096], P('ctx', 'tp'), may hold values from -60 to 60
- w_query: bfloat16 [4096, 4096], P(None, 'tp'), may hold values from -0.09375 to 0.09375
- w_key: bfloat16 [4096, 1024], P(None, 'tp'), may hold values from -0.09375 to 0.09375
- w_value: bfloat16 [4096, 1024], P(None, 'tp'), may hold values from -0.09375 to 0.09375
- w_output: bfloat16 [4096, 4096], P('tp'), may hold values from -0.09375 to 0.09375
- pattern: int32 [128, 8], P('ctx'), may hold values from 0 to 127, as said below
- doc_lengths: int32 [16], replicated, may hold values from 1 to 10240, 16384 in all
Outputs:
- attn_out: bfloat16 [16384, 4096], P(('ctx', 'tp'))
Inputs may be any that keep to these rules, and one draw needn't show every extreme that they name: `pattern`: row q has 8 entries; the first is q itself and every entry is at most q; entries may repeat. The rows of one index of ctx (4 rows) name at most 2 distinct blocks held by any other index of ctx (index i holding blocks i * 4 onward), and exactly 2 of index 0 for every other index. Every row of an index i in the upper half of ctx names 2 blocks of index i minus half the number of ctx indices.
All inputs are finite; a program needn't handle non-finite values.
Results may differ from a plain program's by a relative error of at most 0.02.
Values may be sent and summed in bfloat16 or wider, within the bound.
No kernel may reach another device: no remote copies, remote signals or barrier semaphores. Data moves between devices by JAX's collectives and lax.ppermute only.
A program may use at most 128 MiB of HBM per device.

v0:
```python
import jax
import jax.numpy as jnp
from jax import lax
from jax.sharding import PartitionSpec as P

HD = 128
BLK = 128
LIST = 8
ROPE_BASE = 500000.0
NEG_LARGE = -1e30


def rotate(projected, head_count, positions):
    split_heads = projected.reshape(projected.shape[0], head_count, HD)
    frequency = ROPE_BASE ** (-(jnp.arange(HD // 2, dtype=jnp.float32) * 2.0 / HD))
    angles = positions.astype(jnp.float32)[:, None] * frequency[None, :]
    cosine_table = jnp.cos(angles)[:, None, :]
    sine_table = jnp.sin(angles)[:, None, :]
    front_half = split_heads[..., : HD // 2]
    back_half = split_heads[..., HD // 2 :]
    return jnp.concatenate(
        [
            front_half * cosine_table - back_half * sine_table,
            back_half * cosine_table + front_half * sine_table,
        ],
        axis=-1,
    )


def document_of(positions, doc_lengths):
    ends = jnp.cumsum(doc_lengths)
    return jnp.sum((ends[None, :] <= positions[:, None]).astype(jnp.int32), axis=1)


def fresh_entries(pattern):
    equal = pattern[:, :, None] == pattern[:, None, :]
    earlier = jnp.tril(jnp.ones((LIST, LIST), dtype=bool), -1)
    return jnp.logical_not(jnp.any(equal & earlier[None], axis=2))


def attend_listed(
    query,
    chosen_keys,
    chosen_values,
    pattern,
    positions,
    documents,
    doc_lengths,
    kv_heads,
    group_size,
):
    local_rows = positions.shape[0]
    block_count = local_rows // BLK
    fresh = fresh_entries(pattern)
    offsets_in = jnp.arange(BLK, dtype=jnp.int32)
    key_index = (pattern[:, :, None] * BLK + offsets_in[None, None, :]).reshape(
        block_count, LIST * BLK
    )
    key_ok = jnp.repeat(fresh, BLK, axis=1)
    key_doc = document_of(key_index.reshape(-1), doc_lengths).reshape(key_index.shape)
    block_pos = positions.reshape(block_count, BLK)
    block_doc = documents.reshape(block_count, BLK)
    block_query = query.reshape(block_count, BLK, kv_heads, group_size, HD)
    allowed = (
        (key_index[:, None, :] <= block_pos[:, :, None])
        & (key_doc[:, None, :] == block_doc[:, :, None])
        & key_ok[:, None, :]
    )
    allowed = allowed[:, None, None, :, :]
    scores = jnp.einsum(
        "bqkgd,blkd->bkgql", block_query, chosen_keys, preferred_element_type=jnp.float32
    )
    masked = jnp.where(allowed, scores, NEG_LARGE)
    row_max = jnp.max(masked, axis=-1, keepdims=True)
    weights = jnp.where(allowed, jnp.exp(masked - row_max), 0.0)
    total = jnp.sum(weights, axis=-1)
    mixed = jnp.einsum(
        "bkgql,blkd->bkgqd",
        weights.astype(jnp.bfloat16),
        chosen_values,
        preferred_element_type=jnp.float32,
    )
    mixed = mixed / total[..., None]
    return (
        jnp.transpose(mixed, (0, 3, 1, 2, 4))
        .reshape(local_rows, kv_heads * group_size * HD)
        .astype(jnp.bfloat16)
    )


def on_device(x_tokens, w_query, w_key, w_value, w_output, pattern, doc_lengths):
    features = lax.all_gather(x_tokens, "tp", axis=1, tiled=True)
    local_rows = features.shape[0]
    query_heads = w_query.shape[1] // HD
    kv_heads = w_key.shape[1] // HD
    group_size = query_heads // kv_heads
    block_count = local_rows // BLK
    positions = lax.axis_index("ctx") * local_rows + jnp.arange(local_rows, dtype=jnp.int32)
    query = rotate(
        jnp.dot(features, w_query, preferred_element_type=jnp.float32), query_heads, positions
    ) * HD ** (-0.5)
    query = query.astype(jnp.bfloat16).reshape(local_rows, kv_heads, group_size, HD)
    keys = rotate(jnp.dot(features, w_key, preferred_element_type=jnp.float32), kv_heads, positions)
    keys = keys.astype(jnp.bfloat16).reshape(local_rows, kv_heads * HD)
    values = jnp.dot(features, w_value, preferred_element_type=jnp.float32).astype(jnp.bfloat16)
    documents = document_of(positions, doc_lengths)
    every_key, every_value = (
        lax.all_gather(keys, "ctx", axis=0, tiled=True),
        lax.all_gather(values, "ctx", axis=0, tiled=True),
    )
    offsets_in = jnp.arange(BLK, dtype=jnp.int32)
    key_index = (pattern[:, :, None] * BLK + offsets_in[None, None, :]).reshape(
        block_count, LIST * BLK
    )
    chosen_keys = every_key[key_index].reshape(block_count, LIST * BLK, kv_heads, HD)
    chosen_values = every_value[key_index].reshape(block_count, LIST * BLK, kv_heads, HD)
    attended = attend_listed(
        query,
        chosen_keys,
        chosen_values,
        pattern,
        positions,
        documents,
        doc_lengths,
        kv_heads,
        group_size,
    )
    return lax.psum_scatter(
        jnp.dot(attended, w_output, preferred_element_type=jnp.float32).astype(jnp.bfloat16),
        "tp",
        scatter_dimension=0,
        tiled=True,
    )


def solution(mesh):
    return jax.shard_map(
        on_device,
        mesh=mesh,
        in_specs=(
            P("ctx", "tp"),
            P(None, "tp"),
            P(None, "tp"),
            P(None, "tp"),
            P("tp", None),
            P("ctx", None),
            P(),
        ),
        out_specs=P(("ctx", "tp"), None),
        check_vma=False,
    )
```

profile of v0, /device:TPU:1, one launch (start us, length us, event | category | flops | bytes accessed | tf_op | source)
XLA Modules:
  0.0 297.7 jit_solution(13942825732113829720)
XLA Ops:
  6.5 0.0 copy-start
  6.5 0.0 all-gather.4.cloned.1.call-start
  6.5 0.7 all-gather.4.cloned.1.call-update
  7.3 0.0 all-gather.8.cloned.1.call-start
  7.3 53.2 %all-gather.4.cloned.1.call-done = bf16[512,4096]{1,0:T(8,128)(2,1)} async-done(((bf16[512,1024]{1,0:T(8,128)(2,1)}), bf16[512,4096]{1,0:T(8,128)(2,1)}) %all-gather.4.cloned.1.call-update) | async-done | bytes 4194320 | tf_op jit(solution)/shard_map/all_gather | solution.py:92
  60.5 0.0 copy-done
  60.5 4.1 %convolution_convert_fusion.1 = bf16[512,256]{1,0:T(8,128)(2,1)} fusion(bf16[512,4096]{1,0:T(8,128)(2,1)} %all-gather.4.cloned.1.call-done, bf16[4096,256]{1,0:T(8,128)(2,1)S(1)} %copy-done), kind=kOutput, calls=%fused_computation.19 | convolution fusion | flops 1073872896 | bytes 6553600 | tf_op jit(solution)/shard_map/dot_general | solution.py:105
  64.6 0.0 all-gather.8.cloned.1.call-update
  64.6 0.0 all-gather.6.cloned.1.call-start
  64.7 0.5 multiply_cosine_fusion
  65.2 4.2 %fusion.23 = f32[512,256]{0,1:T(8,128)S(1)} fusion(bf16[512,4096]{1,0:T(8,128)(2,1)} %all-gather.4.cloned.1.call-done, bf16[4096,256]{1,0:T(8,128)(2,1)} %param.9), kind=kOutput, calls=%fused_computation.51 | convolution fusion | flops 1073741824 | bytes 6815744 | tf_op jit(solution)/shard_map/dot_general | solution.py:103
  69.4 0.0 copy-start.4
  69.4 0.0 copy-start.5
  69.4 0.1 subtract_convert_fusion
  69.6 0.9 copy.38
  70.4 0.0 all-gather.6.cloned.1.call-update
  70.4 0.2 reduce-scatter.2.cloned.1.call-start
  70.7 0.1 iota_compare_fusion
  70.8 0.0 copy-done.4
  70.8 0.2 and_reduce_fusion
  71.0 0.1 broadcast_bitcast_fusion.1
  71.1 0.0 copy-done.5
  71.1 0.1 copy.25
  71.2 0.1 reduce
  71.3 0.1 add.112
  71.4 0.1 broadcast_bitcast_fusion
  71.5 0.1 convert_reduce_fusion
  71.7 0.1 convert_reduce_fusion.1
  71.8 3.9 %and_and_fusion = pred[4,128,1024]{1,2,0:T(8,128)(4,1)} fusion(s32[4,128]{1,0:T(4,128)S(1)} %bitcast.60, s32[4,1024]{1,0:T(4,128)S(1)} %eq.34, s32[4,128]{1,0:T(4,128)S(1)} %add_add_fusion, s32[4,1024]{1,0:T(4,128)S(1)} %bitcast_add_fusion, pred[4,1024]{1,0:T(4,128)(4,1)S(1)} %bitcast.59), kind=kLoop, calls=%fused_computation.18 | loop fusion | flops 2097152 | bytes 565248 | tf_op jit(solution)/shard_map/and | solution.py:65
  75.7 8.3 %fusion.24 = f32[512,1024]{0,1:T(8,128)S(1)} fusion(bf16[512,4096]{1,0:T(8,128)(2,1)} %all-gather.4.cloned.1.call-done, bf16[4096,1024]{1,0:T(8,128)(2,1)} %param.8), kind=kOutput, calls=%fused_computation.52 | convolution fusion | flops 4294967296 | bytes 14680064 | tf_op jit(solution)/shard_map/reshape | solution.py:14
  84.0 0.3 multiply_subtract_fusion
  84.3 1.3 concatenate.13
  85.6 1.7 copy.29
  87.4 1.3 concatenate.14
  88.7 2.7 copy.30
  91.4 27.2 %all-gather.8.cloned.1.call-done = bf16[16384,256]{1,0:T(8,128)(2,1)} async-done(((bf16[512,256]{1,0:T(8,128)(2,1)}), bf16[16384,256]{1,0:T(8,128)(2,1)}) %all-gather.8.cloned.1.call-update) | async-done | bytes 8388624 | tf_op jit(solution)/shard_map/all_gather | solution.py:109
  118.6 20.4 %gather_fusion.1 = bf16[4096,256]{1,0:T(8,128)(2,1)} fusion(bf16[16384,256]{1,0:T(8,128)(2,1)} %all-gather.8.cloned.1.call-done, s32[4096]{0:T(1024)S(1)} %bitcast_clamp_fusion), kind=kCustom, calls=%fused_computation.1 | custom fusion | bytes 4210688 | tf_op jit(solution)/shard_map/gather | solution.py:116
  139.0 4.0 %reshape.220 = bf16[4,1024,2,128]{3,2,1,0:T(2,128)(2,1)} reshape(bf16[4096,256]{1,0:T(8,128)(2,1)} %gather_fusion.1) | data formatting | bytes 4194304 | tf_op jit(solution)/shard_map/reshape | solution.py:116
  143.0 30.5 %all-gather.6.cloned.1.call-done = bf16[16384,256]{1,0:T(8,128)(2,1)} async-done(((bf16[512,256]{1,0:T(8,128)(2,1)}), bf16[16384,256]{1,0:T(8,128)(2,1)}) %all-gather.6.cloned.1.call-update) | async-done | bytes 8388624 | tf_op jit(solution)/shard_map/all_gather | solution.py:108
  173.4 20.4 %gather_fusion = bf16[4096,256]{1,0:T(8,128)(2,1)} fusion(bf16[16384,256]{1,0:T(8,128)(2,1)} %all-gather.6.cloned.1.call-done, s32[4096]{0:T(1024)S(1)} %bitcast_clamp_fusion), kind=kCustom, calls=%fused_computation | custom fusion | bytes 4210688 | tf_op jit(solution)/shard_map/gather | solution.py:115
  193.8 4.0 %reshape.218 = bf16[4,1024,2,128]{3,2,1,0:T(2,128)(2,1)} reshape(bf16[4096,256]{1,0:T(8,128)(2,1)} %gather_fusion) | data formatting | bytes 4194304 | tf_op jit(solution)/shard_map/reshape | solution.py:115
  197.8 0.0 copy-start.3
  197.8 10.5 %fusion.9 = f32[4,2,1024,128,4]{3,2,4,1,0:T(8,128)} fusion(bf16[4,1024,2,128,1]{3,2,1,0,4:T(2,128)(2,1)} %bitcast.54, f32[4,128,2,4,64]{4,1,3,2,0:T(8,128)} %copy.30, f32[4,128,2,4,64]{4,1,3,2,0:T(8,128)S(1)} %copy.29), kind=kOutput, calls=%fused_computation.16 | convolution fusion | flops 1075314688 | bytes 20971520 | tf_op jit(solution)/shard_map/bqkgd,blkd->bkgql/dot_general | solution.py:70
  208.3 0.0 copy-done.3
  208.3 0.0 copy-start.2
  208.3 19.6 %fusion.22 = (f32[4,2,4,128]{3,2,1,0:T(4,128)S(1)}, bf16[4,2,4,128,1024]{3,4,2,1,0:T(8,128)(2,1)}) fusion(f32[4,2,1024,128,4]{3,2,4,1,0:T(8,128)} %fusion.9, pred[4,128,1024]{1,2,0:T(8,128)(4,1)S(1)} %copy-done.3), kind=kOutput, calls=%fused_computation.50 | output fusion | flops 25166848 | bytes 25706496 | tf_op jit(solution)/shard_map/sub | solution.py:75
  227.9 0.0 copy-done.2
  227.9 6.2 %fusion.7 = bf16[4,128,2,4,128]{4,1,3,2,0:T(8,128)(2,1)S(1)} fusion(f32[4,128,2,4]{1,3,2,0:T(4,128)S(1)} %bitcast.62, bf16[4,1024,2,128,1]{3,2,1,0,4:T(2,128)(2,1)S(1)} %bitcast.55, bf16[4,2,4,128,1024]{3,4,2,1,0:T(8,128)(2,1)} %get-tuple-element.14), kind=kOutput, calls=%fused_computation.14 | convolution fusion | flops 1074790400 | bytes 11550720 | tf_op jit(solution)/shard_map/bkgql,blkd->bkgqd/dot_general | solution.py:77
  234.1 0.8 copy.34
  234.9 0.8 convert_element_type.46
  235.7 9.4 %convolution_convert_fusion = bf16[512,4096]{1,0:T(8,128)(2,1)} fusion(bf16[512,1024]{1,0:T(8,128)(2,1)S(1)} %convert_element_type.46, bf16[1024,4096]{1,0:T(8,128)(2,1)} %param.11), kind=kOutput, calls=%fused_computation.10 | convolution fusion | flops 4297064448 | bytes 13631488 | tf_op jit(solution)/shard_map/dot_general | solution.py:129
  245.1 0.0 copy-start.1
  245.1 0.0 reduce-scatter.2.cloned.1.call-update
  245.1 46.0 %reduce-scatter.2.cloned.1.call-done = bf16[128,4096]{1,0:T(8,128)(2,1)} async-done(((bf16[512,4096]{1,0:T(8,128)(2,1)}), bf16[128,4096]{1,0:T(8,128)(2,1)}) %reduce-scatter.2.cloned.1.call-update) | async-done | bytes 1048592 | tf_op jit(solution)/shard_map/reduce_scatter | solution.py:128
  291.1 0.0 copy-done.1
  (15 shorter events, 0.2 us)
Async XLA Ops:
  6.5 53.9 %copy-start = (bf16[4096,256]{1,0:T(8,128)(2,1)S(1)}, bf16[4096,256]{1,0:T(8,128)(2,1)}, u32[]{:S(2)}) copy-start(bf16[4096,256]{1,0:T(8,128)(2,1)} %param.10) | copy-start | bytes 6291460
  6.5 53.9 %all-gather.4.cloned.1.call-start = ((), (), s32[]{:S(2)}) async-start(), calls=%async_computation.1 | async-start | bytes 5242880 | tf_op jit(solution)/shard_map/all_gather | solution.py:92
  7.3 111.4 %all-gather.8.cloned.1.call-start = ((), (), s32[]{:S(2)}) async-start(), calls=%async_computation.3 | async-start | bytes 8650752 | tf_op jit(solution)/shard_map/all_gather | solution.py:109
  64.6 108.8 %all-gather.6.cloned.1.call-start = ((), (), s32[]{:S(2)}) async-start(), calls=%async_computation.2 | async-start | bytes 8650752 | tf_op jit(solution)/shard_map/all_gather | solution.py:108
  69.4 1.4 copy-start.4
  69.4 1.7 copy-start.5
  70.4 220.7 %reduce-scatter.2.cloned.1.call-start = ((), (), s32[]{:S(2)}) async-start(), calls=%async_computation.4 | async-start | bytes 5242880 | tf_op jit(solution)/shard_map/reduce_scatter | solution.py:128
  197.8 10.5 %copy-start.3 = (pred[4,128,1024]{1,2,0:T(8,128)(4,1)S(1)}, pred[4,128,1024]{1,2,0:T(8,128)(4,1)}, u32[]{:S(2)}) copy-start(pred[4,128,1024]{1,2,0:T(8,128)(4,1)} %and_and_fusion) | copy-start | bytes 1572868
  208.3 19.6 %copy-start.2 = (bf16[4,1024,2,128]{3,2,1,0:T(2,128)(2,1)S(1)}, bf16[4,1024,2,128]{3,2,1,0:T(2,128)(2,1)}, u32[]{:S(2)}) copy-start(bf16[4,1024,2,128]{3,2,1,0:T(2,128)(2,1)} %reshape.220) | copy-start | bytes 6291460
  245.1 46.1 %copy-start.1 = (bf16[4096,256]{1,0:T(8,128)(2,1)S(1)}, bf16[4096,256]{1,0:T(8,128)(2,1)}, u32[]{:S(2)}) copy-start(bf16[4096,256]{1,0:T(8,128)(2,1)} %param.10) | copy-start | bytes 6291460
Sparse Core Ops, SparseCore 0:
  9.0 51.3 all-gather.3
  64.7 53.8 all-gather.7
  120.9 52.5 all-gather.5
  245.2 45.8 reduce-scatter.1
where the time goes:
time: 298 us
  waiting for transfers between devices  158 us (53%)
  local copies, waits for them, and re-layouts  58.6 us (20%)
  matrix products  42.6 us (14%)
  other arithmetic  25.3 us (8%)
  between operations  13.3 us (4%)
    all_gather x1, waiting for transfers between devices, on_device(): features = lax.all_gather(x_tokens, 'tp', axis=1, tiled=True)  53.2 us
    reduce_scatter x1, waiting for transfers between devices, on_device(): lax.psum_scatter(jnp.dot(attended, w_output, preferred_element_type=jnp.f...  46 us
    all_gather x1, waiting for transfers between devices, on_device(): lax.all_gather(keys, 'ctx', axis=0, tiled=True)  30.5 us
    all_gather x1, waiting for transfers between devices, on_device(): lax.all_gather(values, 'ctx', axis=0, tiled=True)  27.2 us
    gather x1, local copies, waits for them, and re-layouts, on_device(): every_key[key_index].reshape(block_count, LIST * BLK, kv_heads, HD)  20.4 us
    gather x1, local copies, waits for them, and re-layouts, on_device(): every_value[key_index].reshape(block_count, LIST * BLK, kv_heads, HD)  20.4 us
    sub x1, other arithmetic, attend_listed(): weights = jnp.where(allowed, jnp.exp(masked - row_max), 0.0)  19.6 us
    dot_general x1, matrix products, attend_listed(): jnp.einsum('bqkgd,blkd->bkgql', block_query, chosen_keys, preferred_eleme...  10.5 us
  transfers between devices with their start and end apart: 4, of which 4 were waited for; matrix products, arithmetic and copies ran while one was open for 17% of the time, Pallas kernels for 0%

commit v1 on v0

--- a/solution.py
+++ b/solution.py
@@ -89,7 +89,9 @@
 
 
 def on_device(x_tokens, w_query, w_key, w_value, w_output, pattern, doc_lengths):
-    features = lax.all_gather(x_tokens, "tp", axis=1, tiled=True)
+    features = jnp.concatenate(
+        lax.all_to_all(jnp.stack([x_tokens] * lax.axis_size("tp")), "tp", 0, 0), axis=1
+    )
     local_rows = features.shape[0]
     query_heads = w_query.shape[1] // HD
     kv_heads = w_key.shape[1] // HD

time: 298 us -> 320 us (1.074)
  local copies, waits for them, and re-layouts: 58.6 us -> 95.5 us
  waiting for transfers between devices: 158 us -> 139 us
  starting transfers between devices: 0.31 us -> 5.16 us
    all_gather x1 -> x0, waiting for transfers between devices: 53.2 us -> none  [on_device(): features = lax.all_gather(x_tokens, 'tp', axis=1, tiled=True)]
    all_to_all x0 -> x1, waiting for transfers between devices: none -> 44 us  [on_device(): lax.all_to_all(jnp.stack([x_tokens] * lax.axis_size('tp')), 'tp', 0, 0)]
    reshape x0 -> x3, local copies, waits for them, and re-layouts: none -> 17.8 us  [on_device(): jnp.concatenate(lax.all_to_all(jnp.stack([x_tokens] * lax.axis_size('tp')...]
    dot_general x0 -> x2, local copies, waits for them, and re-layouts: none -> 15.4 us  [the longest x1 11.3 us: on_device(): jnp.dot(features, w_query, preferred_element_type=jnp.float32)]
    all_gather x1, waiting for transfers between devices: 30.5 us -> 18.5 us  [on_device(): lax.all_gather(keys, 'ctx', axis=0, tiled=True)]
    reshape x1 -> x0, matrix products: 8.29 us -> none  [rotate(): split_heads = projected.reshape(projected.shape[0], head_count, HD)]
    dot_general x0 -> x1, matrix products: none -> 8.26 us  [on_device(): jnp.dot(features, w_query, preferred_element_type=jnp.float32)]
    all_to_all x0 -> x1, starting transfers between devices: none -> 4.86 us  [on_device(): lax.all_to_all(jnp.stack([x_tokens] * lax.axis_size('tp')), 'tp', 0, 0)]
  transfers between devices with their start and end apart: 4 -> 4, of which waited for: 4 -> 4; matrix products, arithmetic and copies ran while one was open for 17% -> 21% of each run, Pallas kernels for 0% -> 0%
where the time goes in v1:
time: 320 us; the launch traced here: 319 us
  waiting for transfers between devices  139 us (43%)
  local copies, waits for them, and re-layouts  95.5 us (30%)
  matrix products  40.6 us (13%)
  other arithmetic  25.2 us (8%)
  between operations  13.3 us (4%)
  starting transfers between devices  5.16 us (2%)
    reduce_scatter x1, waiting for transfers between devices, on_device(): lax.psum_scatter(jnp.dot(attended, w_output, preferred_element_type=jnp.f...  46.1 us
    all_to_all x1, waiting for transfers between devices, on_device(): lax.all_to_all(jnp.stack([x_tokens] * lax.axis_size('tp')), 'tp', 0, 0)  44 us
    all_gather x1, waiting for transfers between devices, on_device(): lax.all_gather(values, 'ctx', axis=0, tiled=True)  30.6 us
    gather x1, local copies, waits for them, and re-layouts, on_device(): every_key[key_index].reshape(block_count, LIST * BLK, kv_heads, HD)  20.3 us
    gather x1, local copies, waits for them, and re-layouts, on_device(): every_value[key_index].reshape(block_count, LIST * BLK, kv_heads, HD)  20.3 us
    sub x1, other arithmetic, attend_listed(): weights = jnp.where(allowed, jnp.exp(masked - row_max), 0.0)  19.6 us
    all_gather x1, waiting for transfers between devices, on_device(): lax.all_gather(keys, 'ctx', axis=0, tiled=True)  18.5 us
    reshape x3, local copies, waits for them, and re-layouts, on_device(): jnp.concatenate(lax.all_to_all(jnp.stack([x_tokens] * lax.axis_size('tp')...  17.8 us
  transfers between devices with their start and end apart: 4, of which 4 were waited for; matrix products, arithmetic and copies ran while one was open for 21% of the time, Pallas kernels for 0%

profile of v1, /device:TPU:1, one launch (start us, length us, event | category | flops | bytes accessed | tf_op | source)
XLA Modules:
  0.0 318.9 jit_solution(12147322538177579040)
XLA Ops:
  6.5 0.0 copy-start
  6.5 3.9 %stack.2 = bf16[4,512,1024]{2,1,0:T(8,128)(2,1)} broadcast(bf16[512,1024]{1,0:T(8,128)(2,1)} %param.7), dimensions={1,2} | broadcast | bytes 5242880 | tf_op jit(solution)/shard_map/stack | solution.py:93
  10.4 4.9 %all-to-all-start = ((bf16[4,512,1024]{2,1,0:T(8,128)(2,1)}), bf16[4,512,1024]{2,1,0:T(8,128)(2,1)}, u32[]{:S(2)}, u32[]{:S(2)}) async-start(bf16[4,512,1024]{2,1,0:T(8,128)(2,1)} %stack.2), calls=%async_computation | async-start | bytes 8388608 | tf_op jit(solution)/shard_map/all_to_all | solution.py:93
  15.3 0.0 all-gather.3.cloned.1.call-start
  15.3 4.1 %copy.52 = bf16[256,4096]{1,0:T(8,128)(2,1)} copy(bf16[256,4096]{0,1:T(8,128)(2,1)} %bitcast.63) | data formatting | bytes 4194304 | tf_op jit(solution)/shard_map/dot_general | solution.py:105
  19.5 0.5 multiply_cosine_fusion
  20.0 44.0 %all-to-all-done = bf16[4,512,1024]{2,1,0:T(8,128)(2,1)} async-done(((bf16[4,512,1024]{2,1,0:T(8,128)(2,1)}), bf16[4,512,1024]{2,1,0:T(8,128)(2,1)}, u32[]{:S(2)}, u32[]{:S(2)}) %all-to-all-start) | async-done | bytes 4194336 | tf_op jit(solution)/shard_map/all_to_all | solution.py:93
  64.0 7.4 %copy.39 = bf16[512,4,1024]{2,1,0:T(4,128)(2,1)} copy(bf16[512,4,1024]{2,0,1:T(8,128)(2,1)} %bitcast.4) | data formatting | bytes 8388608 | tf_op jit(solution)/shard_map/reshape | solution.py:92
  71.4 7.8 %reshape.247 = bf16[512,4096,1]{1,0,2:T(8,128)(2,1)} reshape(bf16[512,4,1024]{2,1,0:T(4,128)(2,1)} %copy.39) | data formatting | bytes 8388608 | tf_op jit(solution)/shard_map/reshape | solution.py:92
  79.2 4.2 %fusion.23 = f32[512,2,128]{0,2,1:T(8,128)S(1)} fusion(bf16[512,4096,1]{1,0,2:T(8,128)(2,1)} %reshape.247, bf16[2,128,4096]{2,1,0:T(8,128)(2,1)} %bitcast.64), kind=kOutput, calls=%fused_computation.51 | convolution fusion | flops 1073741824 | bytes 6815744 | tf_op jit(solution)/shard_map/dot_general | solution.py:105
  83.4 0.1 subtract_convert_fusion
  83.5 0.8 copy.41
  84.3 0.0 all-gather.3.cloned.1.call-update
  84.4 0.0 all-gather.5.cloned.1.call-start
  84.4 2.6 copy.58
  87.1 0.0 copy-start.4
  87.1 0.0 copy-start.5
  87.1 0.0 copy-done
  87.1 2.0 convolution_convert_fusion.1
  89.1 0.0 all-gather.5.cloned.1.call-update
  89.1 0.2 reduce-scatter.2.cloned.1.call-start
  89.4 0.1 iota_compare_fusion
  89.4 0.0 copy-done.4
  89.4 0.2 and_reduce_fusion
  89.7 0.1 broadcast_bitcast_fusion.1
  89.8 0.0 copy-done.5
  89.8 0.1 copy.38
  89.9 0.1 reduce
  90.0 0.1 add.112
  90.1 0.1 broadcast_bitcast_fusion
  90.2 0.1 convert_reduce_fusion
  90.3 11.3 %copy.55 = bf16[1024,4096]{1,0:T(8,128)(2,1)} copy(bf16[1024,4096]{0,1:T(8,128)(2,1)} %bitcast.59) | data formatting | bytes 16777216 | tf_op jit(solution)/shard_map/dot_general | solution.py:102
  101.6 0.1 convert_reduce_fusion.1
  101.7 3.9 %and_and_fusion = pred[4,128,1024]{1,2,0:T(8,128)(4,1)} fusion(s32[4,128]{1,0:T(4,128)S(1)} %bitcast.68, s32[4,1024]{1,0:T(4,128)S(1)} %eq.34, s32[4,128]{1,0:T(4,128)S(1)} %add_add_fusion, s32[4,1024]{1,0:T(4,128)S(1)} %bitcast_add_fusion, pred[4,1024]{1,0:T(4,128)(4,1)S(1)} %bitcast.67), kind=kLoop, calls=%fused_computation.18 | loop fusion | flops 2097152 | bytes 565248 | tf_op jit(solution)/shard_map/and | solution.py:65
  105.6 8.3 %fusion.24 = f32[512,8,128]{0,2,1:T(8,128)S(1)} fusion(bf16[512,4096,1]{1,0,2:T(8,128)(2,1)} %reshape.247, bf16[8,128,4096]{2,1,0:T(8,128)(2,1)} %bitcast.60), kind=kOutput, calls=%fused_computation.52 | convolution fusion | flops 4294967296 | bytes 14680064 | tf_op jit(solution)/shard_map/dot_general | solution.py:102
  113.9 0.3 multiply_subtract_fusion
  114.2 1.3 concatenate.13
  115.5 1.7 copy.43
  117.3 1.3 concatenate.14
  118.6 2.7 copy.44
  121.3 18.5 %all-gather.3.cloned.1.call-done = bf16[16384,256]{1,0:T(8,128)(2,1)} async-done(((bf16[512,256]{1,0:T(8,128)(2,1)}), bf16[16384,256]{1,0:T(8,128)(2,1)}) %all-gather.3.cloned.1.call-update) | async-done | bytes 8388624 | tf_op jit(solution)/shard_map/all_gather | solution.py:110
  139.8 20.3 %gather_fusion = bf16[4096,256]{1,0:T(8,128)(2,1)} fusion(bf16[16384,256]{1,0:T(8,128)(2,1)} %all-gather.3.cloned.1.call-done, s32[4096]{0:T(1024)S(1)} %bitcast_clamp_fusion), kind=kCustom, calls=%fused_computation | custom fusion | bytes 4210688 | tf_op jit(solution)/shard_map/gather | solution.py:117
  160.0 4.0 %reshape.225 = bf16[4,1024,2,128]{3,2,1,0:T(2,128)(2,1)} reshape(bf16[4096,256]{1,0:T(8,128)(2,1)} %gather_fusion) | data formatting | bytes 4194304 | tf_op jit(solution)/shard_map/reshape | solution.py:117
  164.0 30.6 %all-gather.5.cloned.1.call-done = bf16[16384,256]{1,0:T(8,128)(2,1)} async-done(((bf16[512,256]{1,0:T(8,128)(2,1)}), bf16[16384,256]{1,0:T(8,128)(2,1)}) %all-gather.5.cloned.1.call-update) | async-done | bytes 8388624 | tf_op jit(solution)/shard_map/all_gather | solution.py:111
  194.6 20.3 %gather_fusion.1 = bf16[4096,256]{1,0:T(8,128)(2,1)} fusion(bf16[16384,256]{1,0:T(8,128)(2,1)} %all-gather.5.cloned.1.call-done, s32[4096]{0:T(1024)S(1)} %bitcast_clamp_fusion), kind=kCustom, calls=%fused_computation.1 | custom fusion | bytes 4210688 | tf_op jit(solution)/shard_map/gather | solution.py:118
  214.9 4.0 %reshape.226 = bf16[4,1024,2,128]{3,2,1,0:T(2,128)(2,1)} reshape(bf16[4096,256]{1,0:T(8,128)(2,1)} %gather_fusion.1) | data formatting | bytes 4194304 | tf_op jit(solution)/shard_map/reshape | solution.py:118
  218.9 0.0 copy-start.3
  218.9 10.5 %fusion.9 = f32[4,2,1024,128,4]{3,2,4,1,0:T(8,128)} fusion(bf16[4,1024,2,128,1]{3,2,1,0,4:T(2,128)(2,1)} %bitcast.61, f32[4,128,2,4,64]{4,1,3,2,0:T(8,128)} %copy.44, f32[4,128,2,4,64]{4,1,3,2,0:T(8,128)S(1)} %copy.43), kind=kOutput, calls=%fused_computation.16 | convolution fusion | flops 1075314688 | bytes 20971520 | tf_op jit(solution)/shard_map/bqkgd,blkd->bkgql/dot_general | solution.py:70
  229.3 0.0 copy-done.3
  229.3 0.0 copy-start.2
  229.3 19.6 %fusion.22 = (f32[4,2,4,128]{3,2,1,0:T(4,128)S(1)}, bf16[4,2,4,128,1024]{3,4,2,1,0:T(8,128)(2,1)}) fusion(f32[4,2,1024,128,4]{3,2,4,1,0:T(8,128)} %fusion.9, pred[4,128,1024]{1,2,0:T(8,128)(4,1)S(1)} %copy-done.3), kind=kOutput, calls=%fused_computation.50 | output fusion | flops 25166848 | bytes 25706496 | tf_op jit(solution)/shard_map/sub | solution.py:75
  248.9 0.0 copy-done.2
  248.9 6.2 %fusion.7 = bf16[4,128,2,4,128]{4,1,3,2,0:T(8,128)(2,1)S(1)} fusion(f32[4,128,2,4]{1,3,2,0:T(4,128)S(1)} %bitcast.70, bf16[4,1024,2,128,1]{3,2,1,0,4:T(2,128)(2,1)S(1)} %bitcast.65, bf16[4,2,4,128,1024]{3,4,2,1,0:T(8,128)(2,1)} %get-tuple-element.14), kind=kOutput, calls=%fused_computation.14 | convolution fusion | flops 1074790400 | bytes 11550720 | tf_op jit(solution)/shard_map/bkgql,blkd->bkgqd/dot_general | solution.py:77
  255.1 0.8 copy.48
  256.0 0.8 convert_element_type.46
  256.7 0.0 copy-start.1
  256.7 9.5 %convolution_convert_fusion = bf16[512,4096]{1,0:T(8,128)(2,1)} fusion(bf16[512,1024]{1,0:T(8,128)(2,1)S(1)} %convert_element_type.46, bf16[1024,4096]{1,0:T(8,128)(2,1)} %param.11), kind=kOutput, calls=%fused_computation.10 | convolution fusion | flops 4297064448 | bytes 13631488 | tf_op jit(solution)/shard_map/dot_general | solution.py:131
  266.3 0.0 reduce-scatter.2.cloned.1.call-update
  266.3 46.1 %reduce-scatter.2.cloned.1.call-done = bf16[128,4096]{1,0:T(8,128)(2,1)} async-done(((bf16[512,4096]{1,0:T(8,128)(2,1)}), bf16[128,4096]{1,0:T(8,128)(2,1)}) %reduce-scatter.2.cloned.1.call-update) | async-done | bytes 1048592 | tf_op jit(solution)/shard_map/reduce_scatter | solution.py:130
  312.4 0.0 copy-done.1
  (15 shorter events, 0.2 us)
Async XLA Ops:
  6.5 80.5 %copy-start = (bf16[4096,256]{1,0:T(8,128)(2,1)S(1)}, bf16[4096,256]{1,0:T(8,128)(2,1)}, u32[]{:S(2)}) copy-start(bf16[4096,256]{1,0:T(8,128)(2,1)} %param.10) | copy-start | bytes 6291460
  10.4 53.6 %all-to-all-start = ((bf16[4,512,1024]{2,1,0:T(8,128)(2,1)}), bf16[4,512,1024]{2,1,0:T(8,128)(2,1)}, u32[]{:S(2)}, u32[]{:S(2)}) async-start(bf16[4,512,1024]{2,1,0:T(8,128)(2,1)} %stack.2), calls=%async_computation | async-start | bytes 8388608 | tf_op jit(solution)/shard_map/all_to_all | solution.py:93
  15.3 124.5 %all-gather.3.cloned.1.call-start = ((), (), s32[]{:S(2)}) async-start(), calls=%async_computation.2 | async-start | bytes 8650752 | tf_op jit(solution)/shard_map/all_gather | solution.py:110
  84.4 110.2 %all-gather.5.cloned.1.call-start = ((), (), s32[]{:S(2)}) async-start(), calls=%async_computation.3 | async-start | bytes 8650752 | tf_op jit(solution)/shard_map/all_gather | solution.py:111
  87.1 2.4 copy-start.4
  87.1 2.7 copy-start.5
  89.1 223.2 %reduce-scatter.2.cloned.1.call-start = ((), (), s32[]{:S(2)}) async-start(), calls=%async_computation.4 | async-start | bytes 5242880 | tf_op jit(solution)/shard_map/reduce_scatter | solution.py:130
  218.9 10.5 %copy-start.3 = (pred[4,128,1024]{1,2,0:T(8,128)(4,1)S(1)}, pred[4,128,1024]{1,2,0:T(8,128)(4,1)}, u32[]{:S(2)}) copy-start(pred[4,128,1024]{1,2,0:T(8,128)(4,1)} %and_and_fusion) | copy-start | bytes 1572868
  229.3 19.6 %copy-start.2 = (bf16[4,1024,2,128]{3,2,1,0:T(2,128)(2,1)S(1)}, bf16[4,1024,2,128]{3,2,1,0:T(2,128)(2,1)}, u32[]{:S(2)}) copy-start(bf16[4,1024,2,128]{3,2,1,0:T(2,128)(2,1)} %reshape.226) | copy-start | bytes 6291460
  256.7 55.6 %copy-start.1 = (bf16[4096,256]{1,0:T(8,128)(2,1)S(1)}, bf16[4096,256]{1,0:T(8,128)(2,1)}, u32[]{:S(2)}) copy-start(bf16[4096,256]{1,0:T(8,128)(2,1)} %param.10) | copy-start | bytes 6291460
Sparse Core Ops, SparseCore 0:
  84.5 55.2 all-gather.2
  142.0 52.5 all-gather.4
  266.4 45.8 reduce-scatter.1
